TPU v7x, 256 devices: a whole 4x4x8 slice. The times are simulated.
256 devices in a mesh: section: 8 (over y, z_lo), dp: 32 (over z_hi, x, core).
Axes of the slice: x: 4, y: 4, z: 8 (z_hi: 4, z_lo: 2; z = z_hi * 2 + z_lo), core: 2. Of those that a mesh axis runs over, the one named last changes fastest.
Arguments:
- frames: bfloat16 [4, 32, 128, 2560], P(None, 'dp'), may hold values from -170 to 170
- gains: float32 [8, 2560], P('section'), may hold values from 0.1 to 1.9
- w_shared: bfloat16 [8, 2560, 2560], P('section', 'dp'), may hold values from -0.125 to 0.125
- temper: float32 [8, 20], P('section'), may hold values from 0.25 to 32
Outputs:
- saved: bfloat16 [8, 4, 32, 128, 2560], P('section', None, 'dp')
All inputs are finite; a program needn't handle non-finite values.
Results may differ from a plain program's by a relative error of at most 0.008.
Values may be sent and summed in bfloat16 or wider, within the bound.
A program may use at most 64 MiB of HBM per device.

v0:
```python
import jax
import jax.numpy as jnp
from jax import lax
from jax.sharding import PartitionSpec as P


def passed_along(shard, axis, by):
    count = lax.axis_size(axis)
    pairs = [(i, i + by) for i in range(count) if 0 <= i + by < count]
    return lax.ppermute(shard, axis, pairs)


def swapped(block, axis, apart):
    count = lax.axis_size(axis)
    route = []
    for low in range(count):
        high = low | 1 << apart
        if high != low and high < count:
            route += [(low, high), (high, low)]
    return lax.ppermute(block, axis, route)


def attend_layer(x, gain, weight, temper_row):
    count = x.shape[0]
    frame_count = x.shape[1]
    width = x.shape[2]
    heads = temper_row.shape[0]
    head_size = width // heads
    x_wide = x.astype(jnp.float32)
    scale = lax.rsqrt(jnp.mean(x_wide * x_wide, axis=-1, keepdims=True) + 1e-05)
    normed = (x_wide * scale * gain).astype(jnp.bfloat16)
    proj = jnp.dot(
        normed.reshape(count * frame_count, width), weight, preferred_element_type=jnp.float32
    )
    proj = proj.astype(jnp.bfloat16).reshape(count, frame_count, heads, head_size)
    values = normed.reshape(count, frame_count, heads, head_size)
    scores = jnp.einsum("bqhd,bkhd->bhqk", proj, proj, preferred_element_type=jnp.float32)
    scores = scores * (temper_row / jnp.sqrt(jnp.float32(head_size)))[None, :, None, None]
    rows = lax.broadcasted_iota(jnp.int32, (frame_count, frame_count), 0)
    cols = lax.broadcasted_iota(jnp.int32, (frame_count, frame_count), 1)
    keep = (cols < rows) | (rows == 0) & (cols == 0)
    scores = jnp.where(keep[None, None], scores, jnp.float32(-1e30))
    top = jnp.max(scores, axis=-1, keepdims=True)
    expo = jnp.exp(scores - top)
    weights = (expo / jnp.sum(expo, axis=-1, keepdims=True)).astype(jnp.bfloat16)
    mixed = jnp.einsum("bhqk,bkhd->bqhd", weights, values, preferred_element_type=jnp.float32)
    return (x_wide + mixed.reshape(count, frame_count, width)).astype(jnp.bfloat16)


def local(frames, gains, w_shared, temper):
    sections = lax.axis_size("section")
    place = lax.axis_index("section")
    whole = lax.all_gather(w_shared, "dp", axis=1, tiled=True)[0]
    gain = gains[0]
    temper_row = temper[0]
    micro_count = frames.shape[0]

    def advance(carry, tick):
        incoming, stored = carry
        micro = tick - place
        active = (micro >= 0) & (micro < micro_count)
        slot = jnp.clip(micro, 0, micro_count - 1)
        first = lax.dynamic_index_in_dim(frames, slot, 0, keepdims=False)
        source = jnp.where(place == 0, first, incoming)
        result = lax.cond(
            active,
            lambda v: attend_layer(v, gain, whole, temper_row),
            lambda v: jnp.zeros_like(v),
            source,
        )
        current = lax.dynamic_index_in_dim(stored, slot, 0, keepdims=False)
        stored = lax.dynamic_update_index_in_dim(
            stored, jnp.where(active, result, current), slot, 0
        )
        incoming = passed_along(result, "section", 1)
        return ((incoming, stored), None)

    start = (jnp.zeros_like(frames[0]), jnp.zeros_like(frames))
    ticks = jnp.arange(micro_count + sections - 1, dtype=jnp.int32)
    (incoming, stored), unused = lax.scan(advance, start, ticks)
    levels = sections.bit_length() - 1
    order = list(range(levels))
    for bit in order:
        stored = swapped(stored, "section", bit)
    return stored[None]


def solution(mesh):
    in_specs = (
        P(None, "dp", None, None),
        P("section", None),
        P("section", "dp", None),
        P("section", None),
    )
    out_specs = P("section", None, "dp", None, None)
    return jax.shard_map(local, mesh=mesh, in_specs=in_specs, out_specs=out_specs, check_vma=False)
```

profile of v0, /device:TPU:96, one launch (start us, length us, event | category | flops | bytes accessed | tf_op | source)
XLA Modules:
  0.0 624.9 jit_solution(17368358206003509008)
XLA Ops:
  11.7 99.4 %all-gather.2.cloned.1.call-done = bf16[1,2560,2560]{2,1,0:T(8,128)(2,1)} async-done(((bf16[1,80,2560]{2,1,0:T(8,128)(2,1)}), bf16[1,2560,2560]{2,1,0:T(8,128)(2,1)}) %all-gather.2.cloned.1.call-update) | async-done | bytes 13107216 | tf_op jit(solution)/shard_map/all_gather | solution.py:53
  113.8 305.3 %while.13 = (s32[]{:T(128)}, bf16[1,128,2560]{1,2,0:T(8,128)(2,1)}, bf16[4,1,128,2560]{3,2,0,1:T(8,128)(2,1)}, s32[11]{0:T(128)S(1)}, s32[]{:T(128)}, /*index=5*...) while((s32[]{:T(128)}, bf16[1,128,2560]{1,2,0:T(8,128)(2,1)}, ...), condition=%wide.region_6.7_spmd, body=%wide.region_0.6_spmd.sunk | while | flops 1852099584 | bytes 38098228 | solution.py:80
  123.4 23.8 %collective-permute-done = bf16[1,128,2560]{1,2,0:T(8,128)(2,1)} collective-permute-done((bf16[1,128,2560]{1,2,0:T(8,128)(2,1)}, bf16[1,128,2560]{1,2,0:T(8,128)(2,1)}, u32[]{:S(2)}, u32[]{:S(2)}) %collective-permute-start) | collective-permute-done | bytes 655392 | tf_op jit(solution)/shard_map/while/body/eval_jaxpr/ppermute | solution.py:10
  148.5 13.7 %conditional.2 = (bf16[1,128,2560]{1,2,0:T(8,128)(2,1)}) conditional(s32[]{:T(128)} %convert_element_type.42, () %tuple.35, (pred[]{:T(512)}, bf16[4,1,128,2560]{2,3,1,0:T(8,128)(2,1)}, s32[]{:T(128)}, bf16[1,128,2560]{1,2,0:T(8,128)(2,1)}, f32[1,2560]{1,0:T(1,128)S(1)}, /*index=5*/bf16[2560,2560]{1,0:T(8,128)(2,1)}, f32[20]{0:T(128)S(1)}) %tuple.36), branch_computations={%region_1.1_spmd, %region_2.5_spmd} | conditional | flops 1851771904 | bytes 28267008 | solution.py:65
  167.9 12.9 %collective-permute-done = bf16[1,128,2560]{1,2,0:T(8,128)(2,1)} collective-permute-done((bf16[1,128,2560]{1,2,0:T(8,128)(2,1)}, bf16[1,128,2560]{1,2,0:T(8,128)(2,1)}, u32[]{:S(2)}, u32[]{:S(2)}) %collective-permute-start) | collective-permute-done | bytes 655392 | tf_op jit(solution)/shard_map/while/body/eval_jaxpr/ppermute | solution.py:10
  182.1 13.7 %conditional.2 = (bf16[1,128,2560]{1,2,0:T(8,128)(2,1)}) conditional(s32[]{:T(128)} %convert_element_type.42, () %tuple.35, (pred[]{:T(512)}, bf16[4,1,128,2560]{2,3,1,0:T(8,128)(2,1)}, s32[]{:T(128)}, bf16[1,128,2560]{1,2,0:T(8,128)(2,1)}, f32[1,2560]{1,0:T(1,128)S(1)}, /*index=5*/bf16[2560,2560]{1,0:T(8,128)(2,1)}, f32[20]{0:T(128)S(1)}) %tuple.36), branch_computations={%region_1.1_spmd, %region_2.5_spmd} | conditional | flops 1851771904 | bytes 28267008 | solution.py:65
  184.3 6.6 %convolution_convert_fusion = bf16[128,2560]{1,0:T(8,128)(2,1)S(1)} fusion(bf16[2560,2560]{1,0:T(8,128)(2,1)} %get-tuple-element.123, bf16[1,128,2560]{1,2,0:T(8,128)(2,1)S(1)} %fusion.6), kind=kOutput, calls=%fused_computation.1 | convolution fusion | flops 1678049280 | bytes 14417920 | tf_op jit(solution)/shard_map/while/body/eval_jaxpr/cond/branch_1_fun/dot_general | solution.py:32
  202.7 10.8 %collective-permute-done = bf16[1,128,2560]{1,2,0:T(8,128)(2,1)} collective-permute-done((bf16[1,128,2560]{1,2,0:T(8,128)(2,1)}, bf16[1,128,2560]{1,2,0:T(8,128)(2,1)}, u32[]{:S(2)}, u32[]{:S(2)}) %collective-permute-start) | collective-permute-done | bytes 655392 | tf_op jit(solution)/shard_map/while/body/eval_jaxpr/ppermute | solution.py:10
  214.8 13.7 %conditional.2 = (bf16[1,128,2560]{1,2,0:T(8,128)(2,1)}) conditional(s32[]{:T(128)} %convert_element_type.42, () %tuple.35, (pred[]{:T(512)}, bf16[4,1,128,2560]{2,3,1,0:T(8,128)(2,1)}, s32[]{:T(128)}, bf16[1,128,2560]{1,2,0:T(8,128)(2,1)}, f32[1,2560]{1,0:T(1,128)S(1)}, /*index=5*/bf16[2560,2560]{1,0:T(8,128)(2,1)}, f32[20]{0:T(128)S(1)}) %tuple.36), branch_computations={%region_1.1_spmd, %region_2.5_spmd} | conditional | flops 1851771904 | bytes 28267008 | solution.py:65
  217.1 6.6 %convolution_convert_fusion = bf16[128,2560]{1,0:T(8,128)(2,1)S(1)} fusion(bf16[2560,2560]{1,0:T(8,128)(2,1)} %get-tuple-element.123, bf16[1,128,2560]{1,2,0:T(8,128)(2,1)S(1)} %fusion.6), kind=kOutput, calls=%fused_computation.1 | convolution fusion | flops 1678049280 | bytes 14417920 | tf_op jit(solution)/shard_map/while/body/eval_jaxpr/cond/branch_1_fun/dot_general | solution.py:32
  236.6 9.0 %collective-permute-done = bf16[1,128,2560]{1,2,0:T(8,128)(2,1)} collective-permute-done((bf16[1,128,2560]{1,2,0:T(8,128)(2,1)}, bf16[1,128,2560]{1,2,0:T(8,128)(2,1)}, u32[]{:S(2)}, u32[]{:S(2)}) %collective-permute-start) | collective-permute-done | bytes 655392 | tf_op jit(solution)/shard_map/while/body/eval_jaxpr/ppermute | solution.py:10
  246.9 13.7 %conditional.2 = (bf16[1,128,2560]{1,2,0:T(8,128)(2,1)}) conditional(s32[]{:T(128)} %convert_element_type.42, () %tuple.35, (pred[]{:T(512)}, bf16[4,1,128,2560]{2,3,1,0:T(8,128)(2,1)}, s32[]{:T(128)}, bf16[1,128,2560]{1,2,0:T(8,128)(2,1)}, f32[1,2560]{1,0:T(1,128)S(1)}, /*index=5*/bf16[2560,2560]{1,0:T(8,128)(2,1)}, f32[20]{0:T(128)S(1)}) %tuple.36), branch_computations={%region_1.1_spmd, %region_2.5_spmd} | conditional | flops 1851771904 | bytes 28267008 | solution.py:65
  269.7 8.0 %collective-permute-done = bf16[1,128,2560]{1,2,0:T(8,128)(2,1)} collective-permute-done((bf16[1,128,2560]{1,2,0:T(8,128)(2,1)}, bf16[1,128,2560]{1,2,0:T(8,128)(2,1)}, u32[]{:S(2)}, u32[]{:S(2)}) %collective-permute-start) | collective-permute-done | bytes 655392 | tf_op jit(solution)/shard_map/while/body/eval_jaxpr/ppermute | solution.py:10
  280.0 18.1 %collective-permute-start = (bf16[1,128,2560]{1,2,0:T(8,128)(2,1)}, bf16[1,128,2560]{1,2,0:T(8,128)(2,1)}, u32[]{:S(2)}, u32[]{:S(2)}) collective-permute-start(bf16[1,128,2560]{1,2,0:T(8,128)(2,1)} %get-tuple-element.283), channel_id=1, source_target_pairs={{0,32},{32,64},{64,96},{96,128},{128,160},{160,192},{192,224},{1,3... | collective-permute-start | bytes 1966088 | tf_op jit(solution)/shard_map/while/body/eval_jaxpr/ppermute | solution.py:10
  300.7 8.2 %collective-permute-done = bf16[1,128,2560]{1,2,0:T(8,128)(2,1)} collective-permute-done((bf16[1,128,2560]{1,2,0:T(8,128)(2,1)}, bf16[1,128,2560]{1,2,0:T(8,128)(2,1)}, u32[]{:S(2)}, u32[]{:S(2)}) %collective-permute-start) | collective-permute-done | bytes 655392 | tf_op jit(solution)/shard_map/while/body/eval_jaxpr/ppermute | solution.py:10
  319.1 7.3 %collective-permute-done = bf16[1,128,2560]{1,2,0:T(8,128)(2,1)} collective-permute-done((bf16[1,128,2560]{1,2,0:T(8,128)(2,1)}, bf16[1,128,2560]{1,2,0:T(8,128)(2,1)}, u32[]{:S(2)}, u32[]{:S(2)}) %collective-permute-start) | collective-permute-done | bytes 655392 | tf_op jit(solution)/shard_map/while/body/eval_jaxpr/ppermute | solution.py:10
  328.7 14.3 %collective-permute-start = (bf16[1,128,2560]{1,2,0:T(8,128)(2,1)}, bf16[1,128,2560]{1,2,0:T(8,128)(2,1)}, u32[]{:S(2)}, u32[]{:S(2)}) collective-permute-start(bf16[1,128,2560]{1,2,0:T(8,128)(2,1)} %get-tuple-element.283), channel_id=1, source_target_pairs={{0,32},{32,64},{64,96},{96,128},{128,160},{160,192},{192,224},{1,3... | collective-permute-start | bytes 1966088 | tf_op jit(solution)/shard_map/while/body/eval_jaxpr/ppermute | solution.py:10
  370.5 17.2 %collective-permute-start = (bf16[1,128,2560]{1,2,0:T(8,128)(2,1)}, bf16[1,128,2560]{1,2,0:T(8,128)(2,1)}, u32[]{:S(2)}, u32[]{:S(2)}) collective-permute-start(bf16[1,128,2560]{1,2,0:T(8,128)(2,1)} %get-tuple-element.283), channel_id=1, source_target_pairs={{0,32},{32,64},{64,96},{96,128},{128,160},{160,192},{192,224},{1,3... | collective-permute-start | bytes 1966088 | tf_op jit(solution)/shard_map/while/body/eval_jaxpr/ppermute | solution.py:10
  406.4 12.7 %collective-permute-done = bf16[1,128,2560]{1,2,0:T(8,128)(2,1)} collective-permute-done((bf16[1,128,2560]{1,2,0:T(8,128)(2,1)}, bf16[1,128,2560]{1,2,0:T(8,128)(2,1)}, u32[]{:S(2)}, u32[]{:S(2)}) %collective-permute-start) | collective-permute-done | bytes 655392 | tf_op jit(solution)/shard_map/while/body/eval_jaxpr/ppermute | solution.py:10
  419.0 48.5 %collective-permute-done.1 = bf16[4,1,128,2560]{3,2,0,1:T(8,128)(2,1)S(1)} collective-permute-done((bf16[4,1,128,2560]{3,2,0,1:T(8,128)(2,1)}, bf16[4,1,128,2560]{3,2,0,1:T(8,128)(2,1)S(1)}, u32[]{:S(2)}, u32[]{:S(2)}) %collective-permute-start.1) | collective-permute-done | bytes 2621472 | tf_op jit(solution)/shard_map/ppermute | solution.py:20
  467.6 14.4 %collective-permute-start.2 = (bf16[4,1,128,2560]{3,2,0,1:T(8,128)(2,1)S(1)}, bf16[4,1,128,2560]{3,2,0,1:T(8,128)(2,1)S(1)}, u32[]{:S(2)}, u32[]{:S(2)}) collective-permute-start(bf16[4,1,128,2560]{3,2,0,1:T(8,128)(2,1)S(1)} %collective-permute-done.1), channel_id=1, source_target_pairs={{0,64},{64,0},{32,96},{96,32},{128,192},{192,128},{160,224},{224,1... | collective-permute-start | bytes 7864328 | tf_op jit(solution)/shard_map/ppermute | solution.py:20
  481.9 48.0 %collective-permute-done.2 = bf16[4,1,128,2560]{3,2,0,1:T(8,128)(2,1)S(1)} collective-permute-done((bf16[4,1,128,2560]{3,2,0,1:T(8,128)(2,1)S(1)}, bf16[4,1,128,2560]{3,2,0,1:T(8,128)(2,1)S(1)}, u32[]{:S(2)}, u32[]{:S(2)}) %collective-permute-start.2) | collective-permute-done | bytes 2621472 | tf_op jit(solution)/shard_map/ppermute | solution.py:20
  530.0 38.1 %collective-permute-start.3 = (bf16[4,1,128,2560]{3,2,0,1:T(8,128)(2,1)S(1)}, bf16[4,1,128,2560]{3,2,0,1:T(8,128)(2,1)S(1)}, u32[]{:S(2)}, u32[]{:S(2)}) collective-permute-start(bf16[4,1,128,2560]{3,2,0,1:T(8,128)(2,1)S(1)} %collective-permute-done.2), channel_id=1, source_target_pairs={{0,128},{128,0},{32,160},{160,32},{64,192},{192,64},{96,224},{224,... | collective-permute-start | bytes 7864328 | tf_op jit(solution)/shard_map/ppermute | solution.py:20
  568.1 48.4 %collective-permute-done.3 = bf16[4,1,128,2560]{3,2,0,1:T(8,128)(2,1)S(1)} collective-permute-done((bf16[4,1,128,2560]{3,2,0,1:T(8,128)(2,1)S(1)}, bf16[4,1,128,2560]{3,2,0,1:T(8,128)(2,1)S(1)}, u32[]{:S(2)}, u32[]{:S(2)}) %collective-permute-start.3) | collective-permute-done | bytes 2621472 | tf_op jit(solution)/shard_map/ppermute | solution.py:20
  (153 shorter events, 158.0 us)
Async XLA Ops:
  6.5 104.6 %all-gather.2.cloned.1.call-start = ((), (), s32[]{:S(2)}) async-start(), calls=%async_computation | async-start | bytes 13516800 | tf_op jit(solution)/shard_map/all_gather | solution.py:53
  112.1 1.7 copy-start
  112.1 1.7 copy-start.1
  116.0 31.2 %collective-permute-start = (bf16[1,128,2560]{1,2,0:T(8,128)(2,1)}, bf16[1,128,2560]{1,2,0:T(8,128)(2,1)}, u32[]{:S(2)}, u32[]{:S(2)}) collective-permute-start(bf16[1,128,2560]{1,2,0:T(8,128)(2,1)} %get-tuple-element.283), channel_id=1, source_target_pairs={{0,32},{32,64},{64,96},{96,128},{128,160},{160,192},{192,224},{1,3... | collective-permute-start | bytes 1966088 | tf_op jit(solution)/shard_map/while/body/eval_jaxpr/ppermute | solution.py:10
  162.2 18.6 %collective-permute-start = (bf16[1,128,2560]{1,2,0:T(8,128)(2,1)}, bf16[1,128,2560]{1,2,0:T(8,128)(2,1)}, u32[]{:S(2)}, u32[]{:S(2)}) collective-permute-start(bf16[1,128,2560]{1,2,0:T(8,128)(2,1)} %get-tuple-element.283), channel_id=1, source_target_pairs={{0,32},{32,64},{64,96},{96,128},{128,160},{160,192},{192,224},{1,3... | collective-permute-start | bytes 1966088 | tf_op jit(solution)/shard_map/while/body/eval_jaxpr/ppermute | solution.py:10
  195.8 17.7 %collective-permute-start = (bf16[1,128,2560]{1,2,0:T(8,128)(2,1)}, bf16[1,128,2560]{1,2,0:T(8,128)(2,1)}, u32[]{:S(2)}, u32[]{:S(2)}) collective-permute-start(bf16[1,128,2560]{1,2,0:T(8,128)(2,1)} %get-tuple-element.283), channel_id=1, source_target_pairs={{0,32},{32,64},{64,96},{96,128},{128,160},{160,192},{192,224},{1,3... | collective-permute-start | bytes 1966088 | tf_op jit(solution)/shard_map/while/body/eval_jaxpr/ppermute | solution.py:10
  228.6 17.0 %collective-permute-start = (bf16[1,128,2560]{1,2,0:T(8,128)(2,1)}, bf16[1,128,2560]{1,2,0:T(8,128)(2,1)}, u32[]{:S(2)}, u32[]{:S(2)}) collective-permute-start(bf16[1,128,2560]{1,2,0:T(8,128)(2,1)} %get-tuple-element.283), channel_id=1, source_target_pairs={{0,32},{32,64},{64,96},{96,128},{128,160},{160,192},{192,224},{1,3... | collective-permute-start | bytes 1966088 | tf_op jit(solution)/shard_map/while/body/eval_jaxpr/ppermute | solution.py:10
  260.6 17.1 %collective-permute-start = (bf16[1,128,2560]{1,2,0:T(8,128)(2,1)}, bf16[1,128,2560]{1,2,0:T(8,128)(2,1)}, u32[]{:S(2)}, u32[]{:S(2)}) collective-permute-start(bf16[1,128,2560]{1,2,0:T(8,128)(2,1)} %get-tuple-element.283), channel_id=1, source_target_pairs={{0,32},{32,64},{64,96},{96,128},{128,160},{160,192},{192,224},{1,3... | collective-permute-start | bytes 1966088 | tf_op jit(solution)/shard_map/while/body/eval_jaxpr/ppermute | solution.py:10
  280.0 28.9 %collective-permute-start = (bf16[1,128,2560]{1,2,0:T(8,128)(2,1)}, bf16[1,128,2560]{1,2,0:T(8,128)(2,1)}, u32[]{:S(2)}, u32[]{:S(2)}) collective-permute-start(bf16[1,128,2560]{1,2,0:T(8,128)(2,1)} %get-tuple-element.283), channel_id=1, source_target_pairs={{0,32},{32,64},{64,96},{96,128},{128,160},{160,192},{192,224},{1,3... | collective-permute-start | bytes 1966088 | tf_op jit(solution)/shard_map/while/body/eval_jaxpr/ppermute | solution.py:10
  311.2 15.2 %collective-permute-start = (bf16[1,128,2560]{1,2,0:T(8,128)(2,1)}, bf16[1,128,2560]{1,2,0:T(8,128)(2,1)}, u32[]{:S(2)}, u32[]{:S(2)}) collective-permute-start(bf16[1,128,2560]{1,2,0:T(8,128)(2,1)} %get-tuple-element.283), channel_id=1, source_target_pairs={{0,32},{32,64},{64,96},{96,128},{128,160},{160,192},{192,224},{1,3... | collective-permute-start | bytes 1966088 | tf_op jit(solution)/shard_map/while/body/eval_jaxpr/ppermute | solution.py:10
  328.7 23.7 %collective-permute-start = (bf16[1,128,2560]{1,2,0:T(8,128)(2,1)}, bf16[1,128,2560]{1,2,0:T(8,128)(2,1)}, u32[]{:S(2)}, u32[]{:S(2)}) collective-permute-start(bf16[1,128,2560]{1,2,0:T(8,128)(2,1)} %get-tuple-element.283), channel_id=1, source_target_pairs={{0,32},{32,64},{64,96},{96,128},{128,160},{160,192},{192,224},{1,3... | collective-permute-start | bytes 1966088 | tf_op jit(solution)/shard_map/while/body/eval_jaxpr/ppermute | solution.py:10
  354.6 13.7 %collective-permute-start = (bf16[1,128,2560]{1,2,0:T(8,128)(2,1)}, bf16[1,128,2560]{1,2,0:T(8,128)(2,1)}, u32[]{:S(2)}, u32[]{:S(2)}) collective-permute-start(bf16[1,128,2560]{1,2,0:T(8,128)(2,1)} %get-tuple-element.283), channel_id=1, source_target_pairs={{0,32},{32,64},{64,96},{96,128},{128,160},{160,192},{192,224},{1,3... | collective-permute-start | bytes 1966088 | tf_op jit(solution)/shard_map/while/body/eval_jaxpr/ppermute | solution.py:10
  370.5 25.6 %collective-permute-start = (bf16[1,128,2560]{1,2,0:T(8,128)(2,1)}, bf16[1,128,2560]{1,2,0:T(8,128)(2,1)}, u32[]{:S(2)}, u32[]{:S(2)}) collective-permute-start(bf16[1,128,2560]{1,2,0:T(8,128)(2,1)} %get-tuple-element.283), channel_id=1, source_target_pairs={{0,32},{32,64},{64,96},{96,128},{128,160},{160,192},{192,224},{1,3... | collective-permute-start | bytes 1966088 | tf_op jit(solution)/shard_map/while/body/eval_jaxpr/ppermute | solution.py:10
  398.4 20.7 %collective-permute-start = (bf16[1,128,2560]{1,2,0:T(8,128)(2,1)}, bf16[1,128,2560]{1,2,0:T(8,128)(2,1)}, u32[]{:S(2)}, u32[]{:S(2)}) collective-permute-start(bf16[1,128,2560]{1,2,0:T(8,128)(2,1)} %get-tuple-element.283), channel_id=1, source_target_pairs={{0,32},{32,64},{64,96},{96,128},{128,160},{160,192},{192,224},{1,3... | collective-permute-start | bytes 1966088 | tf_op jit(solution)/shard_map/while/body/eval_jaxpr/ppermute | solution.py:10
  419.0 48.5 %collective-permute-start.1 = (bf16[4,1,128,2560]{3,2,0,1:T(8,128)(2,1)}, bf16[4,1,128,2560]{3,2,0,1:T(8,128)(2,1)S(1)}, u32[]{:S(2)}, u32[]{:S(2)}) collective-permute-start(bf16[4,1,128,2560]{3,2,0,1:T(8,128)(2,1)} %get-tuple-element.137), channel_id=1, source_target_pairs={{0,32},{32,0},{64,96},{96,64},{128,160},{160,128},{192,224},{224,1... | collective-permute-start | bytes 7864328 | tf_op jit(solution)/shard_map/ppermute | solution.py:20
  467.6 62.4 %collective-permute-start.2 = (bf16[4,1,128,2560]{3,2,0,1:T(8,128)(2,1)S(1)}, bf16[4,1,128,2560]{3,2,0,1:T(8,128)(2,1)S(1)}, u32[]{:S(2)}, u32[]{:S(2)}) collective-permute-start(bf16[4,1,128,2560]{3,2,0,1:T(8,128)(2,1)S(1)} %collective-permute-done.1), channel_id=1, source_target_pairs={{0,64},{64,0},{32,96},{96,32},{128,192},{192,128},{160,224},{224,1... | collective-permute-start | bytes 7864328 | tf_op jit(solution)/shard_map/ppermute | solution.py:20
  530.0 86.6 %collective-permute-start.3 = (bf16[4,1,128,2560]{3,2,0,1:T(8,128)(2,1)S(1)}, bf16[4,1,128,2560]{3,2,0,1:T(8,128)(2,1)S(1)}, u32[]{:S(2)}, u32[]{:S(2)}) collective-permute-start(bf16[4,1,128,2560]{3,2,0,1:T(8,128)(2,1)S(1)} %collective-permute-done.2), channel_id=1, source_target_pairs={{0,128},{128,0},{32,160},{160,32},{64,192},{192,64},{96,224},{224,... | collective-permute-start | bytes 7864328 | tf_op jit(solution)/shard_map/ppermute | solution.py:20
Sparse Core Ops, SparseCore 0:
  9.9 101.1 all-gather.1
where the time goes:
time: 626 us; the launch traced here: 625 us
  waiting for transfers between devices  356 us (57%)
  starting transfers between devices  137 us (22%)
  local copies, waits for them, and re-layouts  52.1 us (8%)
  matrix products  34.3 us (5%)
  other arithmetic  24.3 us (4%)
  between operations  13.4 us (2%)
  loops' own time  7.74 us (1%)
    ppermute x3, waiting for transfers between devices, swapped(): return lax.ppermute(block, axis, route)  145 us
    ppermute x11, waiting for transfers between devices, passed_along(): return lax.ppermute(shard, axis, pairs)  111 us
    all_gather x1, waiting for transfers between devices, local(): whole = lax.all_gather(w_shared, 'dp', axis=1, tiled=True)[0]  99.4 us
    ppermute x11, starting transfers between devices, passed_along(): return lax.ppermute(shard, axis, pairs)  84.7 us
    ppermute x3, starting transfers between devices, swapped(): return lax.ppermute(block, axis, route)  52.5 us
    dot_general x4, matrix products, attend_layer(): jnp.dot(normed.reshape(count * frame_count, width), weight, preferred_ele...  26.5 us
    dynamic_slice x22, local copies, waits for them, and re-layouts, advance(): current = lax.dynamic_index_in_dim(stored, slot, 0, keepdims=False)  16 us
  transfers between devices with their start and end apart: 15, of which 15 were waited for; matrix products, arithmetic and copies ran while one was open for 6% of the time, Pallas kernels for 0%

commit v1 on v0

v1 whole, which is shorter than its diff:
```python
import functools

import jax
import jax.numpy as jnp
from jax import lax
from jax.experimental import pallas as pl
from jax.experimental.pallas import tpu as pltpu
from jax.sharding import PartitionSpec as P

MESH = pl.DeviceIdType.MESH
F32 = jnp.float32
BF16 = jnp.bfloat16

D = 2560
FR = 128
LAYERS = 8
PLANES = 4
QD = D // PLANES
HEAD = 128
QH = QD // HEAD
NX = 4
NZH = 4
ROWS = 80


def kernel(
    frames, w_in, gt_in, out,
    w, xs, nrm, gt,
    w1s, w1r, zs, zr, x_s, x_r, cs, cr, ys, yr, gs, gr, fl, ol, os_, or_,
):
    sec = lax.axis_index("section")
    dp = lax.axis_index("dp")
    y = sec // 2
    zl = sec % 2
    zh = dp // 8
    x = (dp // 2) % NX
    c = dp % 2
    z = zh * 2 + zl

    def at_y(q):
        return (q * 2 + zl, dp)

    def at_x(xx):
        return (sec, zh * 8 + xx * 2 + c)

    def at_z(zz):
        return (y * 2 + zz % 2, (zz // 2) * 8 + x * 2 + c)

    sibling = (sec, zh * 8 + x * 2 + 1 - c)
    pair = (y * 2 + 1 - zl, dp)

    peers = [at_y((y + d) % PLANES) for d in range(1, PLANES)]
    peers += [at_x((x + d) % NX) for d in range(1, NX)]
    peers += [at_z((z + d) % 8) for d in range(1, 8)]
    peers += [sibling]
    peers += [(((y + d) % PLANES) * 2 + 1 - zl, dp) for d in range(1, PLANES)]
    barrier = pltpu.get_barrier_semaphore()
    for p in peers:
        pl.semaphore_signal(barrier, inc=1, device_id=p, device_id_type=MESH)
    pl.semaphore_wait(barrier, len(peers))

    def remote(src, dst, s, r, to):
        return pltpu.make_async_remote_copy(
            src_ref=src, dst_ref=dst, send_sem=s, recv_sem=r, device_id=to, device_id_type=MESH
        )

    def w1_copy(d):
        q = (y + d) % PLANES
        return remote(
            w_in.at[0, :, pl.ds(pl.multiple_of(q * QD, QD), QD)],
            w.at[sec, zh, x, c],
            w1s.at[d - 1], w1r.at[d - 1], at_y(q),
        )

    def w1_own():
        return pltpu.make_async_copy(
            w_in.at[0, :, pl.ds(pl.multiple_of(y * QD, QD), QD)], w.at[sec, zh, x, c], w1s.at[3]
        )

    def z_copy(p, d):
        l = 2 * p + zl
        return remote(
            w.at[l, zh, x, c], w.at[l, zh, x, c], zs.at[p, d - 1], zr.at[l, zh], at_z((z + d) % 8)
        )

    def z_arrival(l, h):
        return remote(w.at[l, h, x, c], w.at[l, h, x, c], zs.at[0, 0], zr.at[l, h], pair)

    def x_copy(l, d):
        return remote(
            w.at[l, :, x, c], w.at[l, :, x, c], x_s.at[l, d - 1], x_r.at[l, d - 1], at_x((x + d) % NX)
        )

    def c_copy(l):
        return remote(w.at[l, :, :, c], w.at[l, :, :, c], cs.at[l], cr.at[l], sibling)

    def y_copy(l, u, d):
        return remote(
            xs.at[l, u, y], xs.at[l, u, y], ys.at[l - 1, u, d - 1], yr.at[l - 1, u, d - 1], at_y((y + d) % PLANES)
        )

    def g_copy(j):
        s = (sec + j) % LAYERS
        return remote(gt_in, gt.at[sec], gs.at[j - 1], gr.at[j - 1], (s, dp))

    def frame_copy(u, q):
        return pltpu.make_async_copy(
            frames.at[2 * zl + u, 0, :, pl.ds(q * QD, QD)], xs.at[0, u, q], fl.at[u, q]
        )

    for d in range(1, PLANES):
        w1_copy(d).start()
    w1_own().start()
    for u in range(2):
        for q in range(PLANES):
            frame_copy(u, q).start()
    for j in range(1, LAYERS):
        g_copy(j).start()
    gt[sec] = gt_in[...]

    def w1_to_z(p):
        for d in range(1, PLANES):
            @pl.when((y - d) % PLANES == p)
            def _():
                w1_copy(d).wait_recv()

        @pl.when(y == p)
        def _():
            w1_own().wait()

        for d in range(1, 8):
            z_copy(p, d).start()

    def z_to_x(l):
        for h in range(NZH):
            @pl.when((l % 2 != zl) | (zh != h))
            def _():
                z_arrival(l, h).wait_recv()
        for d in range(1, NX):
            x_copy(l, d).start()

    def x_to_c(l):
        for d in range(1, NX):
            x_copy(l, d).wait_recv()
        c_copy(l).start()

    w1_to_z(0)
    w1_to_z(1)
    z_to_x(0)
    z_to_x(1)
    w1_to_z(2)
    x_to_c(0)
    w1_to_z(3)
    for u in range(2):
        for q in range(PLANES):
            frame_copy(u, q).wait()
    for j in range(1, LAYERS):
        g_copy(j).wait_recv()

    own_saved = LAYERS - 1 - sec
    pair_saved = LAYERS - 1 - pair[0]

    def out_at(ref, m, q):
        return ref.at[0, m, 0, :, pl.ds(q * QD, QD)]

    def own_save(l, u, q):
        return pltpu.make_async_copy(xs.at[l, u, q], out_at(out, 2 * zl + u, q), ol.at[u, q])

    def pair_save(l, u, q):
        return remote(xs.at[l, u, q], out_at(out, 2 * zl + u, q), os_.at[u, q], or_.at[u, q], pair)

    def saves(l, u):
        @pl.when(l == own_saved + 1)
        def _():
            for q in range(PLANES):
                own_save(l, u, q).start()

        @pl.when(l == pair_saved + 1)
        def _():
            for q in range(PLANES):
                pair_save(l, u, q).start()

    rows = lax.broadcasted_iota(jnp.int32, (FR, FR), 0)
    cols = lax.broadcasted_iota(jnp.int32, (FR, FR), 1)
    keep = (cols < rows) | ((rows == 0) & (cols == 0))

    def compute(l, u):
        parts = [xs[l, u, q].astype(F32) for q in range(PLANES)]
        square = sum(jnp.sum(p * p, axis=-1, keepdims=True) for p in parts)
        scale = lax.rsqrt(square * (1.0 / D) + 1e-05)
        for q in range(PLANES):
            nrm[q] = (parts[q] * scale * gt[l, 0:1, q * QD:(q + 1) * QD]).astype(BF16)
        lhs = jnp.concatenate([nrm[q] for q in range(PLANES)], axis=1)
        proj = jnp.dot(lhs, w[l].reshape(D, QD), preferred_element_type=F32).astype(BF16)
        values = nrm[y]
        temper = gt[l, 1:2, pl.ds(pl.multiple_of(y * QD, QD), QD)]
        heads = [proj[:, k * HEAD:(k + 1) * HEAD] for k in range(QH)]
        scores = [
            lax.dot_general(h, h, (((1,), (1,)), ((), ())), preferred_element_type=F32) for h in heads
        ]
        scores = [
            jnp.where(keep, s * temper[:, k * HEAD:(k + 1) * HEAD], -1e30) for k, s in enumerate(scores)
        ]
        tops = [jnp.max(s, axis=-1, keepdims=True) for s in scores]
        expo = [jnp.exp(s - t) for s, t in zip(scores, tops)]
        sums = [jnp.sum(e, axis=-1, keepdims=True) for e in expo]
        weights = [(e / s).astype(BF16) for e, s in zip(expo, sums)]
        mixed = [
            jnp.dot(wt, values[:, k * HEAD:(k + 1) * HEAD], preferred_element_type=F32)
            for k, wt in enumerate(weights)
        ]
        xs[l + 1, u, y] = (xs[l, u, y].astype(F32) + jnp.concatenate(mixed, axis=1)).astype(BF16)

    def layer(l, carry):
        c_copy(l).wait_recv()
        for u in range(2):
            @pl.when(l > 0)
            def _():
                for d in range(1, PLANES):
                    y_copy(l, u, d).wait_recv()
                saves(l, u)

            compute(l, u)
            for d in range(1, PLANES):
                y_copy(l + 1, u, d).start()

        @pl.when(l + 2 < LAYERS)
        def _():
            z_to_x(l + 2)

        @pl.when(l + 1 < LAYERS)
        def _():
            x_to_c(l + 1)

        return carry

    lax.fori_loop(0, LAYERS, layer, 0)

    for u in range(2):
        for d in range(1, PLANES):
            y_copy(LAYERS, u, d).wait_recv()
        saves(LAYERS, u)

    for d in range(1, PLANES):
        w1_copy(d).wait_send()
    for j in range(1, LAYERS):
        g_copy(j).wait_send()
    for p in range(4):
        for d in range(1, 8):
            z_copy(p, d).wait_send()

    def drain(l, carry):
        for d in range(1, NX):
            x_copy(l, d).wait_send()
        c_copy(l).wait_send()
        for u in range(2):
            for d in range(1, PLANES):
                y_copy(l + 1, u, d).wait_send()
        return carry

    lax.fori_loop(0, LAYERS, drain, 0)
    for u in range(2):
        for q in range(PLANES):
            own_save(0, u, q).wait()
            pair_save(0, u, q).wait_send()
            pair_save(0, u, q).wait_recv()


def local(frames, gains, w_shared, temper):
    scale = jnp.repeat(temper * (1.0 / jnp.sqrt(jnp.float32(HEAD))), HEAD, axis=1)
    gt_in = jnp.concatenate([gains, scale], axis=0)
    dma = pltpu.SemaphoreType.DMA
    any_space = pl.BlockSpec(memory_space=pl.ANY)
    return pl.pallas_call(
        kernel,
        out_shape=jax.ShapeDtypeStruct((1,) + frames.shape, BF16),
        in_specs=[any_space, any_space, pl.BlockSpec(memory_space=pltpu.VMEM)],
        out_specs=any_space,
        scratch_shapes=[
            pltpu.VMEM((LAYERS, NZH, NX, 2, ROWS, QD), BF16),
            pltpu.VMEM((LAYERS + 1, 2, PLANES, FR, QD), BF16),
            pltpu.VMEM((PLANES, FR, QD), BF16),
            pltpu.VMEM((LAYERS, 2, D), F32),
            dma((4,)), dma((3,)),
            dma((4, 7)), dma((LAYERS, NZH)),
            dma((LAYERS, 3)), dma((LAYERS, 3)),
            dma((LAYERS,)), dma((LAYERS,)),
            dma((LAYERS, 2, 3)), dma((LAYERS, 2, 3)),
            dma((LAYERS - 1,)), dma((LAYERS - 1,)),
            dma((2, PLANES)), dma((2, PLANES)),
            dma((2, PLANES)), dma((2, PLANES)),
        ],
        compiler_params=pltpu.CompilerParams(
            collective_id=0, has_side_effects=True, vmem_limit_bytes=58 << 20
        ),
    )(frames, w_shared, gt_in)


def solution(mesh):
    in_specs = (
        P(None, "dp", None, None),
        P("section", None),
        P("section", "dp", None),
        P("section", None),
    )
    out_specs = P("section", None, "dp", None, None)
    return jax.shard_map(local, mesh=mesh, in_specs=in_specs, out_specs=out_specs, check_vma=False)
```

time: 626 us -> 231 us (0.37)
  the two profiles are of different devices: /device:TPU:96 before, /device:TPU:33 now
where the time goes in v1:
time: 231 us; the launch traced here: 228 us
  Pallas kernels  222 us (96%)
  local copies, waits for them, and re-layouts  3.49 us (2%)
    pallas_call x1, Pallas kernels, local(): pl.pallas_call(kernel, out_shape=jax.ShapeDtypeStruct((1,) + frames.shape...  222 us

profile of v1, /device:TPU:33, one launch (start us, length us, event | category | flops | bytes accessed | tf_op | source)
XLA Modules:
  0.0 227.9 jit_solution(1828192313799963559)
XLA Ops:
  0.0 0.7 multiply_bitcast_fusion
  0.7 0.1 broadcast_bitcast_fusion
  0.7 1.3 pad_maximum_fusion.gt_in
  2.1 222.5 %shard_map.46 = bf16[1,4,1,128,2560]{4,3,2,1,0:T(8,128)(2,1)} custom-call(bf16[4,1,128,2560]{3,2,1,0:T(8,128)(2,1)} %frames.1, bf16[1,80,2560]{2,1,0:T(8,128)(2,1)} %w_in.1, f32[2,2560]{1,0:T(2,128)} %pad_maximum_fusion.gt_in), custom_call_target="tpu_custom_call" | custom-call | tf_op jit(solution)/shard_map/pallas_call | solution.py:274
  224.5 3.4 %copy.9 = bf16[1,4,1,128,2560]{4,3,2,1,0:T(8,128)(2,1)} copy(bf16[1,4,1,128,2560]{4,3,2,1,0:T(8,128)(2,1)} %shard_map.46) | data formatting | bytes 5242880
  (1 shorter events, 0.0 us)

commit v2 on v1

v2 whole, which is shorter than its diff:
```python
import functools

import jax
import jax.numpy as jnp
from jax import lax
from jax.experimental import pallas as pl
from jax.experimental.pallas import tpu as pltpu
from jax.sharding import PartitionSpec as P

MESH = pl.DeviceIdType.MESH
F32 = jnp.float32
BF16 = jnp.bfloat16

D = 2560
FR = 128
HF = FR // 2
LAYERS = 8
PLANES = 4
QD = D // PLANES
HEAD = 128
QH = QD // HEAD
NX = 4
NZH = 4
ROWS = 80


def kernel(
    frames, w_in, gains, temper_in, out,
    w, shard, xs, nrm, gt,
    w1s, w1r, sl, zs, zr, x1s, x1r, x2s, x2r, ps, pr, cs, cr, y1s, y1r, y2s, y2r, gs, gr, fl, ol, os_, or_, ls, lr, es, er, hs, hr, rr,
):
    sec = lax.axis_index("section")
    dp = lax.axis_index("dp")
    y = sec // 2
    zl = sec % 2
    zh = dp // 8
    x = (dp // 2) % NX
    c = dp % 2
    z = zh * 2 + zl

    def at_y(q):
        return (q * 2 + zl, dp)

    def at_x(xx):
        return (sec, zh * 8 + xx * 2 + c)

    def at_z(zz):
        return (y * 2 + zz % 2, (zz // 2) * 8 + x * 2 + c)

    sibling = (sec, zh * 8 + x * 2 + 1 - c)
    pair = (y * 2 + 1 - zl, dp)

    peers = [at_y((y + d) % PLANES) for d in range(1, PLANES)]
    peers += [at_x((x + 1) % NX), at_x((x + 3) % NX)]
    peers += [at_z((z + d) % 8) for d in range(1, 8)]
    peers += [sibling]
    peers += [(((y + d) % PLANES) * 2 + 1 - zl, dp) for d in range(1, PLANES)]
    barrier = pltpu.get_barrier_semaphore()
    for p in peers:
        pl.semaphore_signal(barrier, inc=1, device_id=p, device_id_type=MESH)
    pl.semaphore_wait(barrier, len(peers))

    def remote(src, dst, s, r, to):
        return pltpu.make_async_remote_copy(
            src_ref=src, dst_ref=dst, send_sem=s, recv_sem=r, device_id=to, device_id_type=MESH
        )

    def w1_copy(d):
        q = (y + d) % PLANES
        return remote(
            w_in.at[0, :, pl.ds(pl.multiple_of(q * QD, QD), QD)],
            shard.at[y],
            w1s.at[d - 1], w1r.at[d - 1], at_y(q),
        )

    def w1_own():
        return pltpu.make_async_copy(
            w_in.at[0, :, pl.ds(pl.multiple_of(y * QD, QD), QD)], shard.at[y], w1s.at[3]
        )

    def shard_copy(p):
        return pltpu.make_async_copy(shard.at[p], w.at[2 * p + zl, zh, x, c], sl.at[p])

    def z_copy(p, d):
        l = 2 * p + zl
        return remote(
            shard.at[p], w.at[l, zh, x, c], zs.at[p, d - 1], zr.at[l, zh], at_z((z + d) % 8)
        )

    def z_arrival(l, h):
        return remote(w.at[l, h, x, c], w.at[l, h, x, c], zs.at[0, 0], zr.at[l, h], pair)

    def x1_copy(l, i):
        return remote(
            w.at[l, :, x, c], w.at[l, :, x, c], x1s.at[l, i], x1r.at[l, i], at_x((x + 1 + 2 * i) % NX)
        )

    def x2_copy(l, i):
        half = w.at[l, 2 * i:2 * i + 2, (x + 3 - 2 * i) % NX, c]
        return remote(half, half, x2s.at[l, i], x2r.at[l, i], at_x((x + 1 + 2 * i) % NX))

    def p_copy(l, i, d):
        part = w.at[l, 2 * i:2 * i + 2, (x + d) % NX, c]
        return remote(
            part, part, ps.at[l // 2, i, d], pr.at[l // 2, i, d], at_z((z + 1 + 6 * i) % 8)
        )

    def c_copy(l, d):
        xx = (x + d) % NX
        return remote(w.at[l, :, xx, c], w.at[l, :, xx, c], cs.at[l, d], cr.at[l, d], sibling)

    def y1_copy(l, u, i):
        return remote(
            xs.at[l, u, y], xs.at[l, u, y], y1s.at[l - 1, u, i], y1r.at[l - 1, u, i],
            at_y((y + 1 + 2 * i) % PLANES),
        )

    def y2_copy(l, u, i):
        half = xs.at[l, u, (y + 3 - 2 * i) % PLANES, i * HF:(i + 1) * HF]
        return remote(
            half, half, y2s.at[l - 1, u, i], y2r.at[l - 1, u, i], at_y((y + 1 + 2 * i) % PLANES)
        )

    def g_copy(j):
        s = (sec + j) % LAYERS
        return remote(gt.at[sec], gt.at[sec], gs.at[j - 1], gr.at[j - 1], (s, dp))

    def frame_copy(u, q):
        return pltpu.make_async_copy(
            frames.at[2 * zl + u, 0, :, pl.ds(q * QD, QD)], xs.at[0, u, q], fl.at[u, q]
        )

    w1_own().start()

    @pl.when(y == 0)
    def _():
        for d in range(1, PLANES):
            w1_copy(d).start()

    for u in range(2):
        for q in range(PLANES):
            frame_copy(u, q).start()
    gt[sec, 0:1] = gains[...]
    tempers = temper_in[...] / (HEAD ** 0.5)
    for k in range(D // HEAD):
        gt[sec, 1:2, k * HEAD:(k + 1) * HEAD] = jnp.broadcast_to(tempers[:, k:k + 1], (1, HEAD))

    works = zl == c

    def z_sends(p, act):
        for d in range(1, 8):
            @pl.when((zl == 1) | (d % 2 == c))
            def _():
                act(z_copy(p, d))

    def w1_arrive(p):
        for d in range(1, PLANES):
            @pl.when((y - d) % PLANES == p)
            def _():
                w1_copy(d).wait_recv()

        @pl.when(y == p)
        def _():
            w1_own().wait()

    def z_issue(p):
        z_sends(p, lambda copy: copy.start())

        @pl.when((zl == 1) | (c == 0))
        def _():
            shard_copy(p).start()

    def w1_to_z(p):
        w1_arrive(p)
        z_issue(p)

    def z_to_x(l):
        @pl.when((l % 2 == 1) | works)
        def _():
            for h in range(NZH):
                @pl.when((l % 2 != zl) | (zh != h))
                def _():
                    z_arrival(l, h).wait_recv()

            @pl.when(l % 2 == zl)
            def _():
                shard_copy(l // 2).wait()

            for i in range(2):
                x1_copy(l, i).start()

    def x1_to_x2(l):
        @pl.when((l % 2 == 1) | works)
        def _():
            for i in range(2):
                x1_copy(l, i).wait_recv()
                x2_copy(l, i).start()

            @pl.when(l % 2 == 0)
            def _():
                for d in (0, 1, 3):
                    for i in range(2):
                        p_copy(l, i, d).start()

            for d in (0, 1, 3):
                c_copy(l, d).start()

    def x2_to_c(l):
        @pl.when((l % 2 == 1) | works)
        def _():
            for i in range(2):
                x2_copy(l, i).wait_recv()

            @pl.when(l % 2 == 0)
            def _():
                for i in range(2):
                    p_copy(l, i, 2).start()

            c_copy(l, 2).start()

        @pl.when((l % 2 == 0) & jnp.logical_not(works))
        def _():
            for d in (0, 1, 3, 2):
                for i in range(2):
                    p_copy(l, i, d).wait_recv()
                c_copy(l, d).start()

    w1_arrive(0)

    @pl.when(zl == 0)
    def _():
        z_issue(0)

    @pl.when(y != 0)
    def _():
        for d in range(1, PLANES):
            w1_copy(d).start()

    for j in range(1, LAYERS):
        g_copy(j).start()
    z_to_x(0)

    @pl.when(zl == 1)
    def _():
        z_issue(0)

    x1_to_x2(0)
    z_to_x(1)
    w1_to_z(1)
    for u in range(2):
        for q in range(PLANES):
            frame_copy(u, q).wait()
    for j in range(1, LAYERS):
        g_copy(j).wait_recv()

    own_saved = LAYERS - 1 - sec
    pair_saved = LAYERS - 1 - pair[0]

    def out_at(ref, m, q):
        return ref.at[0, m, 0, :, pl.ds(q * QD, QD)]

    def own_save(l, u, q):
        return pltpu.make_async_copy(xs.at[l, u, q], out_at(out, 2 * zl + u, q), ol.at[u, q])

    def pair_save(l, u, q):
        return remote(xs.at[l, u, q], out_at(out, 2 * zl + u, q), os_.at[u, q], or_.at[u, q], pair)

    top = xs.at[LAYERS]

    def last_copy(u):
        return remote(
            top.at[u, y],
            out.at[0, 2 * zl + u, 0, :, pl.ds(pl.multiple_of(y * QD, QD), QD)],
            ls.at[u], lr.at[u, zl, y], (0, dp),
        )

    def far_half(u, i):
        half = top.at[u, 2, i * HF:(i + 1) * HF]
        return remote(half, half, hs.at[u, i], hr.at[u], (2 + 4 * i, dp))

    def far_whole(u):
        return remote(top.at[u, 2], top.at[u, 2], ls.at[u], hr.at[u], (1, dp))

    def half_on(u):
        i = y // 2
        part = pl.ds(pl.multiple_of(i * HF, HF), HF)
        return remote(
            top.at[u, 2, part], out.at[0, u, 0, part, 2 * QD:3 * QD], hs.at[u, 0], rr.at[u, i], (0, dp)
        )

    def whole_on(u):
        return remote(top.at[u, 2], out_at(out, 2 + u, 2), hs.at[u, 0], lr.at[u, 1, 2], (0, dp))

    def half_arrival(u, i):
        return remote(
            top.at[u, 2, i * HF:(i + 1) * HF], out.at[0, u, 0, i * HF:(i + 1) * HF, 2 * QD:3 * QD],
            hs.at[u, 0], rr.at[u, i], (1, dp),
        )

    direct = (sec != 0) & (y != 2)
    halves_on = (sec == 2) | (sec == 6)

    def last_own(u):
        return pltpu.make_async_copy(xs.at[LAYERS, u, 0], out_at(out, u, 0), ls.at[u])

    def last_arrival(u, zz, q):
        return remote(
            xs.at[LAYERS, u, q], out_at(out, 2 * zz + u, q), ls.at[u], lr.at[u, zz, q], (1, dp)
        )

    def saves(l, first, last):
        def due(saved):
            return (saved >= first) & (saved <= last) & (l == 6)

        for u in range(2):
            @pl.when(due(own_saved) | (own_saved == 6) & (first == 5) & (l == 7))
            def _():
                for q in range(PLANES):
                    own_save(own_saved + 1, u, q).start()

            @pl.when(due(pair_saved))
            def _():
                for q in range(PLANES):
                    pair_save(pair_saved + 1, u, q).start()

    def late_copy(u):
        return remote(
            xs.at[LAYERS - 1, u, y],
            out.at[0, 2 * zl + u, 0, :, pl.ds(pl.multiple_of(y * QD, QD), QD)],
            es.at[u], er.at[u, y], (1, dp),
        )

    def late_arrival(u, q):
        return remote(
            xs.at[LAYERS - 1, u, q], out_at(out, u, q), es.at[u], er.at[u, q], (0, dp)
        )

    rows = lax.broadcasted_iota(jnp.int32, (FR, FR), 0)
    cols = lax.broadcasted_iota(jnp.int32, (FR, FR), 1)
    keep = (cols < rows) | ((rows == 0) & (cols == 0))

    def compute(l, u):
        parts = [xs[l, u, q].astype(F32) for q in range(PLANES)]
        square = sum(jnp.sum(p * p, axis=-1, keepdims=True) for p in parts)
        scale = lax.rsqrt(square * (1.0 / D) + 1e-05)
        for q in range(PLANES):
            nrm[q] = (parts[q] * scale * gt[l, 0:1, q * QD:(q + 1) * QD]).astype(BF16)
        lhs = jnp.concatenate([nrm[q] for q in range(PLANES)], axis=1)
        proj = jnp.dot(lhs, w[l].reshape(D, QD), preferred_element_type=F32).astype(BF16)
        values = nrm[y]
        temper = gt[l, 1:2, pl.ds(pl.multiple_of(y * QD, QD), QD)]
        heads = [proj[:, k * HEAD:(k + 1) * HEAD] for k in range(QH)]
        scores = [
            lax.dot_general(h, h, (((1,), (1,)), ((), ())), preferred_element_type=F32) for h in heads
        ]
        scores = [
            jnp.where(keep, s * temper[:, k * HEAD:(k + 1) * HEAD], -1e30) for k, s in enumerate(scores)
        ]
        tops = [jnp.max(s, axis=-1, keepdims=True) for s in scores]
        expo = [jnp.exp(s - t) for s, t in zip(scores, tops)]
        sums = [jnp.sum(e, axis=-1, keepdims=True) for e in expo]
        weights = [(e / s).astype(BF16) for e, s in zip(expo, sums)]
        mixed = [
            jnp.dot(wt, values[:, k * HEAD:(k + 1) * HEAD], preferred_element_type=F32)
            for k, wt in enumerate(weights)
        ]
        xs[l + 1, u, y] = (xs[l, u, y].astype(F32) + jnp.concatenate(mixed, axis=1)).astype(BF16)

    def state_in(l, u):
        @pl.when(l > 0)
        def _():
            for i in range(2):
                y1_copy(l, u, i).wait_recv()
                y2_copy(l, u, i).start()

    def step(l, u):
        @pl.when(l > 0)
        def _():
            for i in range(2):
                y2_copy(l, u, i).wait_recv()

        compute(l, u)

        @pl.when((l == LAYERS - 1) & (sec == 0))
        def _():
            last_own(u).start()

        @pl.when((l == LAYERS - 1) & direct)
        def _():
            last_copy(u).start()

        @pl.when((l == LAYERS - 1) & (sec == 4))
        def _():
            for i in range(2):
                far_half(u, i).start()

        @pl.when((l == LAYERS - 1) & (sec == 5))
        def _():
            far_whole(u).start()

        @pl.when(l + 1 < LAYERS)
        def _():
            for i in range(2):
                y1_copy(l + 1, u, i).start()

    def ahead(l):
        @pl.when(l + 2 < LAYERS)
        def _():
            z_to_x(l + 2)

        for p in (2, 3):
            @pl.when(l + 2 == 2 * p - 2)
            def _():
                w1_to_z(p)

    def layer(l, carry):
        x2_to_c(l)
        saves(l, 0, 4)
        state_in(l, 0)

        @pl.when((l > 0) & (l + 1 < LAYERS))
        def _():
            x1_to_x2(l + 1)

        state_in(l, 1)

        @pl.when(l > 0)
        def _():
            ahead(l)

        for d in range(NX):
            c_copy(l, d).wait_recv()
        step(l, 0)

        @pl.when(l == 0)
        def _():
            x1_to_x2(1)

        step(l, 1)

        @pl.when(l == 0)
        def _():
            ahead(0)

        saves(l, 5, 5)
        return carry

    lax.fori_loop(0, LAYERS, layer, 0)

    @pl.when(zl == 0)
    def _():
        for u in range(2):
            late_copy(u).start()

    @pl.when(halves_on)
    def _():
        for u in range(2):
            far_half(u, 0).wait_recv()
            half_on(u).start()

    @pl.when(sec == 1)
    def _():
        for u in range(2):
            far_whole(u).wait_recv()
            whole_on(u).start()

    for d in range(1, PLANES):
        w1_copy(d).wait_send()
    for j in range(1, LAYERS):
        g_copy(j).wait_send()
    for p in range(4):
        z_sends(p, lambda copy: copy.wait_send())

    def drain(l, carry):
        @pl.when((l % 2 == 1) | works)
        def _():
            for i in range(2):
                x1_copy(l, i).wait_send()
                x2_copy(l, i).wait_send()

        @pl.when((l % 2 == 0) & works)
        def _():
            for i in range(2):
                for d in range(NX):
                    p_copy(l, i, d).wait_send()

        for d in range(NX):
            c_copy(l, d).wait_send()

        @pl.when(l > 0)
        def _():
            for u in range(2):
                for i in range(2):
                    y1_copy(l, u, i).wait_send()
                    y2_copy(l, u, i).wait_send()

        return carry

    lax.fori_loop(0, LAYERS, drain, 0)

    @pl.when(sec != 0)
    def _():
        for u in range(2):
            for q in range(PLANES):
                own_save(0, u, q).wait()

    @pl.when(direct)
    def _():
        for u in range(2):
            last_copy(u).wait_send()

    @pl.when(sec == 4)
    def _():
        for u in range(2):
            for i in range(2):
                far_half(u, i).wait_send()

    @pl.when(sec == 5)
    def _():
        for u in range(2):
            far_whole(u).wait_send()

    @pl.when(halves_on)
    def _():
        for u in range(2):
            half_on(u).wait_send()

    @pl.when(sec == 1)
    def _():
        for u in range(2):
            whole_on(u).wait_send()

    @pl.when(sec > 1)
    def _():
        for u in range(2):
            for q in range(PLANES):
                pair_save(0, u, q).wait_send()
                pair_save(0, u, q).wait_recv()

    @pl.when(zl == 0)
    def _():
        for u in range(2):
            late_copy(u).wait_send()

    @pl.when(sec == 1)
    def _():
        for u in range(2):
            for q in range(PLANES):
                late_arrival(u, q).wait_recv()

    @pl.when(sec == 0)
    def _():
        for u in range(2):
            last_own(u).wait()
            for zz in range(2):
                for q in range(PLANES):
                    if (zz, q) not in ((0, 0), (0, 2)):
                        last_arrival(u, zz, q).wait_recv()
            for i in range(2):
                half_arrival(u, i).wait_recv()


def local(frames, gains, w_shared, temper):
    dma = pltpu.SemaphoreType.DMA
    any_space = pl.BlockSpec(memory_space=pl.ANY)
    return pl.pallas_call(
        kernel,
        out_shape=jax.ShapeDtypeStruct((1,) + frames.shape, BF16),
        in_specs=[any_space, any_space] + [pl.BlockSpec(memory_space=pltpu.VMEM)] * 2,
        out_specs=any_space,
        scratch_shapes=[
            pltpu.VMEM((LAYERS, NZH, NX, 2, ROWS, QD), BF16),
            pltpu.VMEM((PLANES, ROWS, QD), BF16),
            pltpu.VMEM((LAYERS + 1, 2, PLANES, FR, QD), BF16),
            pltpu.VMEM((PLANES, FR, QD), BF16),
            pltpu.VMEM((LAYERS, 2, D), F32),
            dma((4,)), dma((3,)), dma((4,)),
            dma((4, 7)), dma((LAYERS, NZH)),
            dma((LAYERS, 2)), dma((LAYERS, 2)),
            dma((LAYERS, 2)), dma((LAYERS, 2)),
            dma((LAYERS // 2, 2, NX)), dma((LAYERS // 2, 2, NX)),
            dma((LAYERS, 4)), dma((LAYERS, 4)),
            dma((LAYERS, 2, 2)), dma((LAYERS, 2, 2)),
            dma((LAYERS, 2, 2)), dma((LAYERS, 2, 2)),
            dma((LAYERS - 1,)), dma((LAYERS - 1,)),
            dma((2, PLANES)), dma((2, PLANES)),
            dma((2, PLANES)), dma((2, PLANES)),
            dma((2,)), dma((2, 2, PLANES)),
            dma((2,)), dma((2, PLANES)),
            dma((2, 2)), dma((2,)), dma((2, 2)),
        ],
        compiler_params=pltpu.CompilerParams(
            collective_id=0, has_side_effects=True, vmem_limit_bytes=58 << 20
        ),
    )(frames, w_shared, gains, temper)


def solution(mesh):
    in_specs = (
        P(None, "dp", None, None),
        P("section", None),
        P("section", "dp", None),
        P("section", None),
    )
    out_specs = P("section", None, "dp", None, None)
    return jax.shard_map(local, mesh=mesh, in_specs=in_specs, out_specs=out_specs, check_vma=False)
```

time: 231 us -> 191 us (0.83)
  the two profiles are of different devices: /device:TPU:33 before, /device:TPU:2 now
where the time goes in v2:
time: 191 us
  Pallas kernels  188 us (98%)
  local copies, waits for them, and re-layouts  3.4 us (2%)
    pallas_call x1, Pallas kernels, local(): pl.pallas_call(kernel, out_shape=jax.ShapeDtypeStruct((1,) + frames.shape...  188 us

profile of v2, /device:TPU:2, one launch (start us, length us, event | category | flops | bytes accessed | tf_op | source)
XLA Modules:
  0.0 191.3 jit_solution(10558033974057503544)
XLA Ops:
  0.0 187.9 %shard_map.46 = bf16[1,4,1,128,2560]{4,3,2,1,0:T(8,128)(2,1)} custom-call(bf16[4,1,128,2560]{3,2,1,0:T(8,128)(2,1)} %frames.1, bf16[1,80,2560]{2,1,0:T(8,128)(2,1)} %w_in.1, f32[1,2560]{1,0:T(1,128)} %gains.1, f32[1,20]{1,0:T(1,128)} %temper_in.1), custom_call_target="tpu_custom_call" | custom-call | tf_op jit(solution)/shard_map/pallas_call | solution.py:566
  187.9 3.4 %copy.6 = bf16[1,4,1,128,2560]{4,3,2,1,0:T(8,128)(2,1)} copy(bf16[1,4,1,128,2560]{4,3,2,1,0:T(8,128)(2,1)} %shard_map.46) | data formatting | bytes 5242880

commit v3 on v2

--- a/solution.py
+++ b/solution.py
@@ -27,7 +27,7 @@
 def kernel(
     frames, w_in, gains, temper_in, out,
     w, shard, xs, nrm, gt,
-    w1s, w1r, sl, zs, zr, x1s, x1r, x2s, x2r, ps, pr, cs, cr, y1s, y1r, y2s, y2r, gs, gr, fl, ol, os_, or_, ls, lr, es, er, hs, hr, rr,
+    w1s, w1r, sl, zs, zr, x1s, x1r, x2s, x2r, ps, pr, cs, cr, y1s, y1r, y2s, y2r, gs, gr, fl, ol, os_, or_, ls, lr, es, er, hs, hr, rr, fr,
 ):
     sec = lax.axis_index("section")
     dp = lax.axis_index("dp")
@@ -279,7 +279,10 @@
         return remote(half, half, hs.at[u, i], hr.at[u], (2 + 4 * i, dp))
 
     def far_whole(u):
-        return remote(top.at[u, 2], top.at[u, 2], ls.at[u], hr.at[u], (1, dp))
+        return remote(top.at[u, 2], top.at[u, 3], ls.at[u], fr.at[u], (2, dp))
+
+    def near_whole(u):
+        return remote(top.at[u, 1], top.at[u, 1], ls.at[u], fr.at[u], (1, dp))
 
     def half_on(u):
         i = y // 2
@@ -288,8 +291,11 @@
             top.at[u, 2, part], out.at[0, u, 0, part, 2 * QD:3 * QD], hs.at[u, 0], rr.at[u, i], (0, dp)
         )
 
-    def whole_on(u):
-        return remote(top.at[u, 2], out_at(out, 2 + u, 2), hs.at[u, 0], lr.at[u, 1, 2], (0, dp))
+    def far_on(u):
+        return remote(top.at[u, 3], out_at(out, 2 + u, 2), hs.at[u, 1], lr.at[u, 1, 2], (0, dp))
+
+    def near_on(u):
+        return remote(top.at[u, 1], out_at(out, 2 + u, 1), hs.at[u, 1], lr.at[u, 1, 1], (0, dp))
 
     def half_arrival(u, i):
         return remote(
@@ -297,7 +303,7 @@
             hs.at[u, 0], rr.at[u, i], (1, dp),
         )
 
-    direct = (sec != 0) & (y != 2)
+    direct = (sec == 1) | (sec == 2) | (sec > 5)
     halves_on = (sec == 2) | (sec == 6)
 
     def last_own(u):
@@ -398,6 +404,10 @@
         def _():
             far_whole(u).start()
 
+        @pl.when((l == LAYERS - 1) & (sec == 3))
+        def _():
+            near_whole(u).start()
+
         @pl.when(l + 1 < LAYERS)
         def _():
             for i in range(2):
@@ -423,11 +433,6 @@
             x1_to_x2(l + 1)
 
         state_in(l, 1)
-
-        @pl.when(l > 0)
-        def _():
-            ahead(l)
-
         for d in range(NX):
             c_copy(l, d).wait_recv()
         step(l, 0)
@@ -436,33 +441,34 @@
         def _():
             x1_to_x2(1)
 
+        ahead(l)
+
+        @pl.when((l == LAYERS - 1) & (zl == 0))
+        def _():
+            for u in range(2):
+                late_copy(u).start()
+
         step(l, 1)
-
-        @pl.when(l == 0)
-        def _():
-            ahead(0)
-
         saves(l, 5, 5)
         return carry
 
     lax.fori_loop(0, LAYERS, layer, 0)
 
-    @pl.when(zl == 0)
-    def _():
-        for u in range(2):
-            late_copy(u).start()
-
-    @pl.when(halves_on)
-    def _():
-        for u in range(2):
+    for u in range(2):
+        @pl.when(halves_on)
+        def _():
             far_half(u, 0).wait_recv()
             half_on(u).start()
 
-    @pl.when(sec == 1)
-    def _():
-        for u in range(2):
+        @pl.when(sec == 2)
+        def _():
             far_whole(u).wait_recv()
-            whole_on(u).start()
+            far_on(u).start()
+
+        @pl.when(sec == 1)
+        def _():
+            near_whole(u).wait_recv()
+            near_on(u).start()
 
     for d in range(1, PLANES):
         w1_copy(d).wait_send()
@@ -520,6 +526,16 @@
         for u in range(2):
             far_whole(u).wait_send()
 
+    @pl.when(sec == 3)
+    def _():
+        for u in range(2):
+            near_whole(u).wait_send()
+
+    @pl.when(sec == 2)
+    def _():
+        for u in range(2):
+            far_on(u).wait_send()
+
     @pl.when(halves_on)
     def _():
         for u in range(2):
@@ -528,7 +544,7 @@
     @pl.when(sec == 1)
     def _():
         for u in range(2):
-            whole_on(u).wait_send()
+            near_on(u).wait_send()
 
     @pl.when(sec > 1)
     def _():
@@ -587,7 +603,7 @@
             dma((2, PLANES)), dma((2, PLANES)),
             dma((2,)), dma((2, 2, PLANES)),
             dma((2,)), dma((2, PLANES)),
-            dma((2, 2)), dma((2,)), dma((2, 2)),
+            dma((2, 2)), dma((2,)), dma((2, 2)), dma((2,)),
         ],
         compiler_params=pltpu.CompilerParams(
             collective_id=0, has_side_effects=True, vmem_limit_bytes=58 << 20

time: 191 us -> 184 us (0.963)
  the two profiles are of different devices: /device:TPU:2 before, /device:TPU:33 now
where the time goes in v3:
time: 184 us
  Pallas kernels  181 us (98%)
  local copies, waits for them, and re-layouts  3.4 us (2%)
    pallas_call x1, Pallas kernels, local(): pl.pallas_call(kernel, out_shape=jax.ShapeDtypeStruct((1,) + frames.shape...  181 us

profile of v3, /device:TPU:33, one launch (start us, length us, event | category | flops | bytes accessed | tf_op | source)
XLA Modules:
  0.0 184.3 jit_solution(17235108274614857083)
XLA Ops:
  0.0 180.9 %shard_map.46 = bf16[1,4,1,128,2560]{4,3,2,1,0:T(8,128)(2,1)} custom-call(bf16[4,1,128,2560]{3,2,1,0:T(8,128)(2,1)} %frames.1, bf16[1,80,2560]{2,1,0:T(8,128)(2,1)} %w_in.1, f32[1,2560]{1,0:T(1,128)} %gains.1, f32[1,20]{1,0:T(1,128)} %temper_in.1), custom_call_target="tpu_custom_call" | custom-call | tf_op jit(solution)/shard_map/pallas_call | solution.py:582
  180.9 3.4 %copy.6 = bf16[1,4,1,128,2560]{4,3,2,1,0:T(8,128)(2,1)} copy(bf16[1,4,1,128,2560]{4,3,2,1,0:T(8,128)(2,1)} %shard_map.46) | data formatting | bytes 5242880

commit v4 on v3

--- a/solution.py
+++ b/solution.py
@@ -109,10 +109,11 @@
         xx = (x + d) % NX
         return remote(w.at[l, :, xx, c], w.at[l, :, xx, c], cs.at[l, d], cr.at[l, d], sibling)
 
-    def y1_copy(l, u, i):
-        return remote(
-            xs.at[l, u, y], xs.at[l, u, y], y1s.at[l - 1, u, i], y1r.at[l - 1, u, i],
-            at_y((y + 1 + 2 * i) % PLANES),
+    def y1_copy(l, u, i, k):
+        h = i if k == 0 else 1 - i
+        part = xs.at[l, u, y, h * HF:(h + 1) * HF]
+        return remote(
+            part, part, y1s.at[l - 1, u, i, k], y1r.at[l - 1, u, i, k], at_y((y + 1 + 2 * i) % PLANES)
         )
 
     def y2_copy(l, u, i):
@@ -376,13 +377,14 @@
         @pl.when(l > 0)
         def _():
             for i in range(2):
-                y1_copy(l, u, i).wait_recv()
+                y1_copy(l, u, i, 0).wait_recv()
                 y2_copy(l, u, i).start()
 
     def step(l, u):
         @pl.when(l > 0)
         def _():
             for i in range(2):
+                y1_copy(l, u, i, 1).wait_recv()
                 y2_copy(l, u, i).wait_recv()
 
         compute(l, u)
@@ -411,7 +413,11 @@
         @pl.when(l + 1 < LAYERS)
         def _():
             for i in range(2):
-                y1_copy(l + 1, u, i).start()
+                y1_copy(l + 1, u, i, 0).start()
+            if u == 1:
+                for v in range(2):
+                    for i in range(2):
+                        y1_copy(l + 1, v, i, 1).start()
 
     def ahead(l):
         @pl.when(l + 2 < LAYERS)
@@ -435,18 +441,19 @@
         state_in(l, 1)
         for d in range(NX):
             c_copy(l, d).wait_recv()
-        step(l, 0)
-
-        @pl.when(l == 0)
-        def _():
-            x1_to_x2(1)
-
-        ahead(l)
 
         @pl.when((l == LAYERS - 1) & (zl == 0))
         def _():
             for u in range(2):
                 late_copy(u).start()
+
+        step(l, 0)
+
+        @pl.when(l == 0)
+        def _():
+            x1_to_x2(1)
+
+        ahead(l)
 
         step(l, 1)
         saves(l, 5, 5)
@@ -497,7 +504,8 @@
         def _():
             for u in range(2):
                 for i in range(2):
-                    y1_copy(l, u, i).wait_send()
+                    for k in range(2):
+                        y1_copy(l, u, i, k).wait_send()
                     y2_copy(l, u, i).wait_send()
 
         return carry
@@ -596,7 +604,7 @@
             dma((LAYERS, 2)), dma((LAYERS, 2)),
             dma((LAYERS // 2, 2, NX)), dma((LAYERS // 2, 2, NX)),
             dma((LAYERS, 4)), dma((LAYERS, 4)),
-            dma((LAYERS, 2, 2)), dma((LAYERS, 2, 2)),
+            dma((LAYERS, 2, 2, 2)), dma((LAYERS, 2, 2, 2)),
             dma((LAYERS, 2, 2)), dma((LAYERS, 2, 2)),
             dma((LAYERS - 1,)), dma((LAYERS - 1,)),
             dma((2, PLANES)), dma((2, PLANES)),

time: 184 us -> 186 us (1.011)
  no operation moved by 1% of the time
where the time goes in v4:
time: 186 us; the launch traced here: 185 us
  Pallas kernels  182 us (98%)
  local copies, waits for them, and re-layouts  3.4 us (2%)
    pallas_call x1, Pallas kernels, local(): pl.pallas_call(kernel, out_shape=jax.ShapeDtypeStruct((1,) + frames.shape...  182 us

profile of v4, /device:TPU:33, one launch (start us, length us, event | category | flops | bytes accessed | tf_op | source)
XLA Modules:
  0.0 185.5 jit_solution(7625074297345521883)
XLA Ops:
  0.0 182.1 %shard_map.46 = bf16[1,4,1,128,2560]{4,3,2,1,0:T(8,128)(2,1)} custom-call(bf16[4,1,128,2560]{3,2,1,0:T(8,128)(2,1)} %frames.1, bf16[1,80,2560]{2,1,0:T(8,128)(2,1)} %w_in.1, f32[1,2560]{1,0:T(1,128)} %gains.1, f32[1,20]{1,0:T(1,128)} %temper_in.1), custom_call_target="tpu_custom_call" | custom-call | tf_op jit(solution)/shard_map/pallas_call | solution.py:590
  182.1 3.4 %copy.6 = bf16[1,4,1,128,2560]{4,3,2,1,0:T(8,128)(2,1)} copy(bf16[1,4,1,128,2560]{4,3,2,1,0:T(8,128)(2,1)} %shard_map.46) | data formatting | bytes 5242880

commit v5 on v3

--- a/solution.py
+++ b/solution.py
@@ -335,6 +335,12 @@
             out.at[0, 2 * zl + u, 0, :, pl.ds(pl.multiple_of(y * QD, QD), QD)],
             es.at[u], er.at[u, y], (1, dp),
         )
+
+    def late_far(u):
+        return remote(xs.at[LAYERS - 1, u, 2], xs.at[LAYERS, u, 0], es.at[u], fr.at[u], (7, dp))
+
+    def late_on(u):
+        return remote(xs.at[LAYERS, u, 0], out_at(out, u, 2), hs.at[u, 1], er.at[u, 2], (1, dp))
 
     def late_arrival(u, q):
         return remote(
@@ -443,10 +449,15 @@
 
         ahead(l)
 
-        @pl.when((l == LAYERS - 1) & (zl == 0))
-        def _():
-            for u in range(2):
-                late_copy(u).start()
+        @pl.when((l == LAYERS - 1) & (zl == 0) & (y != 2))
+        def _():
+            for v in range(2):
+                late_copy(v).start()
+
+        @pl.when((l == LAYERS - 1) & (sec == 4))
+        def _():
+            for v in range(2):
+                late_far(v).start()
 
         step(l, 1)
         saves(l, 5, 5)
@@ -455,6 +466,11 @@
     lax.fori_loop(0, LAYERS, layer, 0)
 
     for u in range(2):
+        @pl.when(sec == 7)
+        def _():
+            late_far(u).wait_recv()
+            late_on(u).start()
+
         @pl.when(halves_on)
         def _():
             far_half(u, 0).wait_recv()
@@ -553,10 +569,20 @@
                 pair_save(0, u, q).wait_send()
                 pair_save(0, u, q).wait_recv()
 
-    @pl.when(zl == 0)
+    @pl.when((zl == 0) & (y != 2))
     def _():
         for u in range(2):
             late_copy(u).wait_send()
+
+    @pl.when(sec == 4)
+    def _():
+        for u in range(2):
+            late_far(u).wait_send()
+
+    @pl.when(sec == 7)
+    def _():
+        for u in range(2):
+            late_on(u).wait_send()
 
     @pl.when(sec == 1)
     def _():

time: 184 us -> 185 us (level)
  no operation moved by 1% of the time
where the time goes in v5:
time: 185 us
  Pallas kernels  181 us (98%)
  local copies, waits for them, and re-layouts  3.4 us (2%)
    pallas_call x1, Pallas kernels, local(): pl.pallas_call(kernel, out_shape=jax.ShapeDtypeStruct((1,) + frames.shape...  181 us

profile of v5, /device:TPU:33, one launch (start us, length us, event | category | flops | bytes accessed | tf_op | source)
XLA Modules:
  0.0 184.7 jit_solution(2623799193468588009)
XLA Ops:
  0.0 181.3 %shard_map.46 = bf16[1,4,1,128,2560]{4,3,2,1,0:T(8,128)(2,1)} custom-call(bf16[4,1,128,2560]{3,2,1,0:T(8,128)(2,1)} %frames.1, bf16[1,80,2560]{2,1,0:T(8,128)(2,1)} %w_in.1, f32[1,2560]{1,0:T(1,128)} %gains.1, f32[1,20]{1,0:T(1,128)} %temper_in.1), custom_call_target="tpu_custom_call" | custom-call | tf_op jit(solution)/shard_map/pallas_call | solution.py:608
  181.3 3.4 %copy.6 = bf16[1,4,1,128,2560]{4,3,2,1,0:T(8,128)(2,1)} copy(bf16[1,4,1,128,2560]{4,3,2,1,0:T(8,128)(2,1)} %shard_map.46) | data formatting | bytes 5242880
